TPU v7x, 256 devices: a whole 4x4x8 slice. The times are simulated.
256 devices in a mesh: row: 8 (over z), col: 32 (over y, x, core).
Axes of the slice: x: 4, y: 4, z: 8, core: 2. Of those that a mesh axis runs over, the one named last changes fastest.
Arguments:
- image_emb: bfloat16 [20480, 1152], P(('row', 'col')), may hold values from -0.19150809 to 0.19150809
- text_emb: bfloat16 [20480, 1152], P(('row', 'col')), may hold values from -0.19150809 to 0.19150809
- logit_scale: float32 [1], replicated, may hold values from 5 to 20
- logit_bias: float32 [1], replicated, may hold values from -6 to -1
Outputs:
- loss_rows: float32 [20480], P(('row', 'col'))
- image_grad: float32 [20480, 1152], P(('row', 'col'))
- text_grad: float32 [20480, 1152], P(('row', 'col'))
- scalar_grads: float32 [2], replicated
All inputs are finite; a program needn't handle non-finite values.
Results may differ from a plain program's by a relative error of at most 0.00093.
Values may be sent and summed in bfloat16 or wider, within the bound.
No kernel may reach another device: no remote copies, remote signals or barrier semaphores. Data moves between devices by JAX's collectives and lax.ppermute only.
A program may use at most 64 MiB of HBM per device.

v0:
```python
import jax
import jax.numpy as jnp
from jax import lax
from jax.sharding import PartitionSpec as P


def normalize(emb):
    values = emb.astype(jnp.float32)
    inverse = lax.rsqrt(jnp.sum(values * values, axis=1, keepdims=True) + 1e-06)
    unit = values * inverse
    return (unit, inverse, unit.astype(jnp.bfloat16))


def body(image_emb, text_emb, logit_scale, logit_bias):
    col_count = lax.axis_size("col")
    scale = logit_scale[0]
    bias = logit_bias[0]
    text_own = text_emb.shape[0]
    image_unit, image_inv, image_local = normalize(image_emb)
    text_unit, text_inv, text_local = normalize(text_emb)
    image_full = lax.all_gather(image_emb, "col", axis=0, tiled=True)
    text_full = lax.all_gather(text_emb, "row", axis=0, tiled=True)
    image_norm = normalize(image_full)[2]
    text_norm = normalize(text_full)[2]
    image_rows = image_norm.shape[0]
    text_rows = text_norm.shape[0]
    total_pairs = text_rows * col_count
    cosine = jnp.einsum("id,jd->ij", image_norm, text_norm, preferred_element_type=jnp.float32)
    logits = scale * cosine + bias
    row_ids = lax.axis_index("row") * image_rows + jnp.arange(image_rows, dtype=jnp.int32)
    positions = jnp.arange(text_rows, dtype=jnp.int32)
    block_ids = positions // text_own
    col_ids = (block_ids * col_count + lax.axis_index("col")) * text_own + positions % text_own
    sign = jnp.where(row_ids[:, None] == col_ids[None, :], 1.0, -1.0).astype(jnp.float32)
    term = jax.nn.softplus(-sign * logits)
    row_part = jnp.sum(term, axis=1) / total_pairs
    dlogit = -sign * jax.nn.sigmoid(-sign * logits)
    sum_cos, sum_plain = lax.psum((jnp.sum(dlogit * cosine), jnp.sum(dlogit)), ("row", "col"))
    denom = jnp.float32(total_pairs) * jnp.float32(total_pairs)
    scalar_grads = jnp.stack([sum_cos, sum_plain]) / denom
    weights = (scale * dlogit).astype(jnp.bfloat16)
    text_part = jnp.einsum("ij,id->jd", weights, image_norm, preferred_element_type=jnp.float32)
    text_share = lax.psum_scatter(text_part, "row", scatter_dimension=0, tiled=True)
    text_grad = text_inv * (
        text_share - text_unit * jnp.sum(text_unit * text_share, axis=1, keepdims=True)
    )
    image_part = jnp.dot(weights, text_norm, preferred_element_type=jnp.float32)
    loss_rows, grad_rows = (
        lax.psum_scatter(row_part, "col", scatter_dimension=0, tiled=True),
        lax.psum_scatter(image_part, "col", scatter_dimension=0, tiled=True),
    )
    image_grad = image_inv * (
        grad_rows - image_unit * jnp.sum(image_unit * grad_rows, axis=1, keepdims=True)
    )
    return (loss_rows, image_grad, text_grad, scalar_grads)


def solution(mesh):
    return jax.shard_map(
        body,
        mesh=mesh,
        in_specs=(P(("row", "col"), None), P(("row", "col"), None), P(), P()),
        out_specs=(P(("row", "col")), P(("row", "col"), None), P(("row", "col"), None), P()),
        check_vma=False,
    )
```

profile of v0, /device:TPU:32, one launch (start us, length us, event | category | flops | bytes accessed | tf_op | source)
XLA Modules:
  0.0 363.8 jit_solution(4428788219550941081)
XLA Ops:
  7.2 0.0 all-gather.5.cloned.1.call-start
  7.2 0.7 all-gather.5.cloned.1.call-update
  7.9 0.0 all-gather.3.cloned.1.call-start
  7.9 0.7 all-gather.3.cloned.1.call-update
  8.6 0.0 reduce-scatter.5.cloned.1.call-start
  10.0 41.8 %all-gather.5.cloned.1.call-done = bf16[640,1152]{1,0:T(8,128)(2,1)} async-done(((bf16[80,1152]{1,0:T(8,128)(2,1)}), bf16[640,1152]{1,0:T(8,128)(2,1)}) %all-gather.5.cloned.1.call-update) | async-done | bytes 1474576 | tf_op jit(solution)/shard_map/all_gather | solution.py:22
  51.8 1.8 fusion.3
  53.7 53.2 %all-gather.3.cloned.1.call-done = bf16[2560,1152]{1,0:T(8,128)(2,1)} async-done(((bf16[80,1152]{1,0:T(8,128)(2,1)}), bf16[2560,1152]{1,0:T(8,128)(2,1)}) %all-gather.3.cloned.1.call-update) | async-done | bytes 5898256 | tf_op jit(solution)/shard_map/all_gather | solution.py:21
  106.9 4.0 %fusion = f32[2560]{0:T(1024)S(1)} fusion(bf16[2560,1152]{1,0:T(8,128)(2,1)} %all-gather.3.cloned.1.call-done), kind=kLoop, calls=%fused_computation.3 | loop fusion | flops 8844800 | bytes 5908480 | tf_op jit(solution)/shard_map/reduce_sum | solution.py:9
  111.0 0.0 copy-done.2
  111.0 0.0 slice-start.1
  111.0 13.5 %multiply_reduce_fusion = (f32[]{:T(128)}, f32[2560]{0:T(1024)S(1)}, f32[]{:T(128)}, f32[2560,640]{0,1:T(8,128)S(1)}) fusion(f32[]{:T(128)} %bitcast.8, f32[]{:T(128)} %bitcast.6, s32[640]{0:T(1024)S(1)} %fusion.33, s32[2560]{0:T(1024)S(1)} %iota_add_fusion, bf16[640,1152]{1,0:T(8,128)(2,1)S(1)} %copy-done.2, f32[640]{0:T(1024)S(1)} %add_rsqrt_fusion.1, ...), kind=kOutput, calls=%fused_computation.6 | convolution fusion | flops 3818698240 | bytes 13962256 | tf_op jit(solution)/shard_map/id,jd->ij/dot_general | solution.py:28
  124.5 2.7 copy-done.4
  127.2 0.0 slice-done
  127.2 0.0 slice-done.1
  127.2 6.4 %fusion.5 = f32[640,1152]{1,0:T(8,128)} fusion(bf16[2560,1152]{1,0:T(8,128)(2,1)S(1)} %bitcast.10, f32[2560]{0:T(1024)S(1)} %add_rsqrt_fusion, f32[2560,640]{0,1:T(8,128)S(1)} %get-tuple-element.9, f32[]{:T(128)} %bitcast.5), kind=kOutput, calls=%fused_computation.15 | convolution fusion | flops 3786997760 | bytes 15411204 | tf_op jit(solution)/shard_map/ij,id->jd/dot_general | solution.py:42
  133.6 0.0 reduce-scatter.5.cloned.1.call-update
  133.6 0.0 reduce-scatter.3.cloned.1.call-start
  133.7 10.0 %fusion.9 = f32[2560,1152]{1,0:T(8,128)} fusion(f32[2560,640]{0,1:T(8,128)} %copy-done.4, f32[]{:T(128)} %bitcast.7, bf16[640,1152]{1,0:T(8,128)(2,1)S(1)} %copy-done.2, f32[640]{0:T(1024)S(1)} %add_rsqrt_fusion.1), kind=kOutput, calls=%fused_computation.17 | convolution fusion | flops 3780362240 | bytes 19827204 | tf_op jit(solution)/shard_map/dot_general | solution.py:47
  143.7 0.0 reduce-scatter.3.cloned.1.call-update
  143.7 0.7 copy-done.3
  144.4 0.6 dynamic-slice
  145.6 0.1 fusion.22
  145.8 0.1 fusion.23
  145.9 76.6 %all-reduce.1 = (f32[1]{0:T(128)}, f32[1]{0:T(128)}) all-reduce(f32[1]{0:T(128)} %bitcast.3, f32[1]{0:T(128)} %bitcast.2), channel_id=1, replica_groups=mesh['row'=8,'col'=32] {'row','col'}, use_global_device_ids=true, to_apply=%region_13.14 | all-reduce | flops 2 | bytes 16 | tf_op jit(solution)/shard_map/psum | solution.py:38
  222.5 126.1 %all-reduce = f32[2560]{0:T(1024)S(1)} all-reduce(f32[2560]{0:T(1024)S(1)} %broadcast_multiply_fusion), channel_id=2, replica_groups=mesh['row'=8,'col'=32] {'col'}, use_global_device_ids=true, to_apply=%region_3.0.clone | all-reduce | flops 2560 | bytes 20480
  348.7 0.6 dynamic-slice.1
  349.3 1.9 maximum_multiply_fusion
  351.1 1.2 fusion.16
  352.4 1.9 fusion.18
  354.2 1.2 fusion.19
  355.4 1.9 fusion.21
  (18 shorter events, 0.1 us)
Async XLA Ops:
  7.2 44.7 %all-gather.5.cloned.1.call-start = ((), (), s32[]{:S(2)}) async-start(), calls=%async_computation.3 | async-start | bytes 1658880 | tf_op jit(solution)/shard_map/all_gather | solution.py:22
  7.9 99.0 %all-gather.3.cloned.1.call-start = ((), (), s32[]{:S(2)}) async-start(), calls=%async_computation.2 | async-start | bytes 6082560 | tf_op jit(solution)/shard_map/all_gather | solution.py:21
  8.6 342.5 %reduce-scatter.5.cloned.1.call-start = ((), (), s32[]{:S(2)}) async-start(), calls=%async_computation.5 | async-start | bytes 3317760 | tf_op jit(solution)/shard_map/reduce_scatter | solution.py:43
  51.8 59.1 %copy-start.2 = (bf16[640,1152]{1,0:T(8,128)(2,1)S(1)}, bf16[640,1152]{1,0:T(8,128)(2,1)}, u32[]{:S(2)}) copy-start(bf16[640,1152]{1,0:T(8,128)(2,1)} %all-gather.5.cloned.1.call-done) | copy-start | bytes 4423684
  106.9 20.3 %slice-start = ((s8[5898240]{0:T(1024)(128)(4,1)}), s8[4194304]{0:T(1024)(128)(4,1)S(1)}, s32[]{:S(2)}) async-start(s8[5898240]{0:T(1024)(128)(4,1)} %bitcast.9), calls=%async_computation.6 | async-start | bytes 8388608
  111.0 16.3 %slice-start.1 = ((s8[5898240]{0:T(1024)(128)(4,1)}), s8[1703936]{0:T(1024)(128)(4,1)S(1)}, s32[]{:S(2)}) async-start(s8[5898240]{0:T(1024)(128)(4,1)} %bitcast.9), calls=%async_computation.7 | async-start | bytes 3407872
  124.5 2.7 copy-start.4
  133.6 220.6 %reduce-scatter.3.cloned.1.call-start = ((), (), s32[]{:S(2)}) async-start(), calls=%async_computation.4 | async-start | bytes 12165120 | tf_op jit(solution)/shard_map/reduce_scatter | solution.py:50
  143.7 0.7 copy-start.3
  143.7 1.9 copy-start.1
  143.7 2.1 copy-start
Sparse Core Ops, SparseCore 0:
  9.8 41.9 all-gather.4
  54.5 52.4 all-gather.2
  133.8 43.7 reduce-scatter.4
  182.0 110.1 reduce-scatter.2
where the time goes:
time: 364 us
  blocking collectives  203 us (56%)
  waiting for transfers between devices  96.4 us (26%)
  matrix products  29.9 us (8%)
  between operations  15.8 us (4%)
  other arithmetic  14.2 us (4%)
  local copies, waits for them, and re-layouts  4.58 us (1%)
    unnamed x1, blocking collectives  126 us
    psum x1, blocking collectives, body(): lax.psum((jnp.sum(dlogit * cosine), jnp.sum(dlogit)), ('row', 'col'))  76.6 us
    all_gather x1, waiting for transfers between devices, body(): image_full = lax.all_gather(image_emb, 'col', axis=0, tiled=True)  53.2 us
    all_gather x1, waiting for transfers between devices, body(): text_full = lax.all_gather(text_emb, 'row', axis=0, tiled=True)  41.8 us
    dot_general x1, matrix products, body(): jnp.einsum('id,jd->ij', image_norm, text_norm, preferred_element_type=jnp...  13.5 us
    dot_general x1, matrix products, body(): image_part = jnp.dot(weights, text_norm, preferred_element_type=jnp.float32)  10 us
  transfers between devices with their start and end apart: 4, of which 2 were waited for; matrix products, arithmetic and copies ran while one was open for 5% of the time, Pallas kernels for 0%

commit v1 on v0

v1 whole, which is shorter than its diff:
```python
import jax
import jax.numpy as jnp
from jax import lax
from jax.experimental import pallas as pl
from jax.experimental.pallas import tpu as pltpu
from jax.sharding import PartitionSpec as P

NZ, NY, NX, NC = 8, 4, 4, 2
SHRINK = 0.125


def normalize(emb):
    values = emb.astype(jnp.float32)
    inverse = lax.rsqrt(jnp.sum(values * values, axis=1, keepdims=True) + 1e-06)
    unit = values * inverse
    return (unit, inverse, unit.astype(jnp.bfloat16))


def send_z(x, d):
    return lax.ppermute(x, "row", [(i, (i + d) % NZ) for i in range(NZ)])


def send_plane(x, dy, dx, dc):
    pairs = []
    for y in range(NY):
        for x_ in range(NX):
            for c in range(NC):
                src = (y * NX + x_) * NC + c
                dst = (((y + dy) % NY) * NX + (x_ + dx) % NX) * NC + (c + dc) % NC
                pairs.append((src, dst))
    return lax.ppermute(x, "col", pairs)


def send_y(x, d):
    return send_plane(x, d, 0, 0)


def send_x(x, d):
    return send_plane(x, 0, d, 0)


def swap(x):
    return send_plane(x, 0, 0, 1)


def narrow(x):
    return (x * SHRINK).astype(jnp.float16)


def widen(x):
    return x.astype(jnp.float32) * (1.0 / SHRINK)


def pair_kernel(own, total, sc_ref, img_ref, txt_ref, gi_ref, gt_ref, loss_ref, sums_ref):
    step = pl.program_id(0)
    scale = sc_ref[0]
    bias = sc_ref[1]
    img = img_ref[...]
    txt = txt_ref[...]
    rows, cols = img.shape[0], txt.shape[0]
    cosine = lax.dot_general(
        img, txt, (((1,), (1,)), ((), ())), preferred_element_type=jnp.float32
    )
    logits = scale * cosine + bias
    half = own // 2
    r = lax.broadcasted_iota(jnp.int32, (rows, 128), 0) + step * rows
    c = lax.broadcasted_iota(jnp.int32, (rows, 128), 1)
    split = (pl.num_programs(0) * rows) // 2
    match = ((r == c) & (r < half)) | ((r - split == c - half) & (c >= half) & (c < own))
    sign = jnp.where(match, -1.0, 1.0)
    head = sign * logits[:, :128]
    signed = jnp.concatenate([head, logits[:, 128:]], axis=1)
    e = jnp.exp(signed)
    p = 1.0 + e
    d = e / p
    d = jnp.concatenate([sign * d[:, :128], d[:, 128:]], axis=1)
    acc = None
    k = 0
    while k < cols:
        q = p[:, k : k + 128]
        for m in range(1, 4):
            if k + 128 * m < cols:
                q = q * p[:, k + 128 * m : k + 128 * (m + 1)]
        q = jnp.log(q)
        acc = q if acc is None else acc + q
        k += 512
    loss_ref[...] = jnp.sum(acc, axis=1, keepdims=True) / total
    sums = jnp.concatenate(
        [
            jnp.sum(d * cosine, axis=0, keepdims=True),
            jnp.sum(d, axis=0, keepdims=True),
        ],
        axis=0,
    )
    w = (scale * d).astype(jnp.bfloat16)
    gi_ref[...] = jnp.dot(w, txt, preferred_element_type=jnp.float32)
    gt = lax.dot_general(w, img, (((0,), (0,)), ((), ())), preferred_element_type=jnp.float32)

    @pl.when(step == 0)
    def _():
        gt_ref[...] = gt
        sums_ref[...] = sums

    @pl.when(step > 0)
    def _():
        gt_ref[...] += gt
        sums_ref[...] += sums


def pairs_block(images, texts, scale, bias, own, total):
    rows, width = images.shape
    cols = texts.shape[0]
    tile = rows // 5
    return pl.pallas_call(
        lambda *refs: pair_kernel(own, total, *refs),
        grid=(rows // tile,),
        in_specs=[
            pl.BlockSpec(memory_space=pltpu.SMEM),
            pl.BlockSpec((tile, width), lambda i: (i, 0)),
            pl.BlockSpec((cols, width), lambda i: (0, 0)),
        ],
        out_specs=[
            pl.BlockSpec((tile, width), lambda i: (i, 0)),
            pl.BlockSpec((cols, width), lambda i: (0, 0)),
            pl.BlockSpec((tile, 1), lambda i: (i, 0)),
            pl.BlockSpec((2, cols), lambda i: (0, 0)),
        ],
        out_shape=[
            jax.ShapeDtypeStruct((rows, width), jnp.float32),
            jax.ShapeDtypeStruct((cols, width), jnp.float32),
            jax.ShapeDtypeStruct((rows, 1), jnp.float32),
            jax.ShapeDtypeStruct((2, cols), jnp.float32),
        ],
        compiler_params=pltpu.CompilerParams(vmem_limit_bytes=48 * 1024 * 1024),
        name="pair_block",
    )(jnp.stack([scale, bias]), images, texts)


def body(image_emb, text_emb, logit_scale, logit_bias):
    scale = logit_scale[0]
    bias = logit_bias[0]
    own = text_emb.shape[0]
    half = own // 2
    total_pairs = own * NZ * NY * NX * NC
    image_unit, image_inv, image_local = normalize(image_emb)
    text_unit, text_inv, text_local = normalize(text_emb)

    t_up = send_z(text_local, -1)
    t_down = send_z(text_local, 1)
    t_far = send_z(text_local, 4)
    a = image_local[:half]
    b = image_local[half:]
    a1 = jnp.concatenate([a] + [send_y(a, -i) for i in range(1, NY)], axis=0)
    b1 = jnp.concatenate([b] + [send_x(b, -i) for i in range(1, NX)], axis=0)
    t_up2 = send_z(jnp.concatenate([t_up, t_far], axis=0), -1)
    t_down2 = send_z(jnp.concatenate([t_down, t_far], axis=0), 1)
    a2 = [a1] + [send_x(a1, -i) for i in range(1, NX)]
    b2 = [b1] + [send_y(b1, -i) for i in range(1, NY)]
    texts_core = jnp.concatenate([text_local, t_up, t_down, t_far, t_up2, t_down2], axis=0)
    texts = jnp.concatenate([texts_core, swap(texts_core)], axis=0)
    images = jnp.concatenate(a2 + b2, axis=0)

    gi, gt, loss, sums = pairs_block(images, texts, scale, bias, own, float(total_pairs))

    sums = lax.psum(jnp.sum(sums, axis=1), ("row", "col"))
    denom = jnp.float32(total_pairs) * jnp.float32(total_pairs)
    scalar_grads = sums / denom

    n = own * NZ
    gt_core = gt[:n] + widen(swap(narrow(gt[n:])))
    pieces = [gt_core[i * own : (i + 1) * own] for i in range(NZ)]
    up = send_z(narrow(jnp.concatenate([pieces[4], pieces[5]], axis=0)), 1)
    down = send_z(narrow(jnp.concatenate([pieces[6], pieces[7]], axis=0)), -1)
    up = widen(up)
    down = widen(down)
    p_up = pieces[1] + up[:own]
    p_down = pieces[2] + down[:own]
    p_far = pieces[3] + up[own:] + down[own:]
    text_share = (
        pieces[0]
        + widen(send_z(narrow(p_up), 1))
        + widen(send_z(narrow(p_down), -1))
        + widen(send_z(narrow(p_far), 4))
    )

    def reduce_two(g, first, second):
        g = g.reshape(4, 4 * half, g.shape[1])
        s = g[0]
        for i in range(1, 4):
            s = s + widen(first(narrow(g[i]), i))
        s = s.reshape(4, half, g.shape[2])
        t = s[0]
        for i in range(1, 4):
            t = t + widen(second(narrow(s[i]), i))
        return t

    m = gi.shape[0] // 2
    image_share = jnp.concatenate(
        [reduce_two(gi[:m], send_x, send_y), reduce_two(gi[m:], send_y, send_x)], axis=0
    )
    la = loss[:m, 0].reshape(NX, NY, half)
    lb = loss[m:, 0].reshape(NY, NX, half)
    col = lax.axis_index("col")
    y0 = col // (NX * NC)
    x0 = col // NC % NX
    c0 = col % NC
    la = jnp.roll(la.transpose(1, 0, 2), (y0, x0), (0, 1))
    lb = jnp.roll(lb, (y0, x0), (0, 1))
    both = jnp.concatenate([la, lb], axis=2)
    both = jnp.where(
        jnp.arange(NC)[None, None, :, None] == c0, both[:, :, None, :], 0.0
    ).reshape(-1)
    loss_rows = lax.psum_scatter(both, "col", scatter_dimension=0, tiled=True)

    text_grad = text_inv * (
        text_share - text_unit * jnp.sum(text_unit * text_share, axis=1, keepdims=True)
    )
    image_grad = image_inv * (
        image_share - image_unit * jnp.sum(image_unit * image_share, axis=1, keepdims=True)
    )
    return (loss_rows, image_grad, text_grad, scalar_grads)


def solution(mesh):
    return jax.shard_map(
        body,
        mesh=mesh,
        in_specs=(P(("row", "col"), None), P(("row", "col"), None), P(), P()),
        out_specs=(P(("row", "col")), P(("row", "col"), None), P(("row", "col"), None), P()),
        check_vma=False,
    )
```

time: 364 us -> 369 us (1.014); the launches traced: 364 us -> 365 us
  waiting for transfers between devices: 96.4 us -> 39.5 us
  starting transfers between devices: 0.16 us -> 53.1 us
  matrix products: 29.9 us -> 0 us
  Pallas kernels: 0 us -> 23.3 us
  between operations: 15.8 us -> 2.97 us
  local copies, waits for them, and re-layouts: 4.58 us -> 14.5 us
  other arithmetic: 14.2 us -> 23.6 us
  blocking collectives: 203 us -> 208 us
    all_gather x2 -> x0, waiting for transfers between devices: 95 us -> none  [the longest x1 53.2 us: body(): image_full = lax.all_gather(image_emb, 'col', axis=0, tiled=True)]
    ppermute x0 -> x36, starting transfers between devices: none -> 53.1 us  [the longest x26 34.4 us: send_plane(): return lax.ppermute(x, 'col', pairs)]
    ppermute x0 -> x36, waiting for transfers between devices: none -> 39.5 us  [the longest x10 21.3 us: send_z(): return lax.ppermute(x, 'row', [(i, (i + d) % NZ) for i in range(NZ)])]
    dot_general x3 -> x0, matrix products: 29.9 us -> none  [the longest x1 13.5 us: body(): jnp.einsum('id,jd->ij', image_norm, text_norm, preferred_element_type=jnp...]
    pallas_call x0 -> x1, Pallas kernels: none -> 23.3 us  [pairs_block(): pl.pallas_call(lambda *refs: pair_kernel(own, total, *refs), grid=(rows /...]
    add x2 -> x5, other arithmetic: 0.02 us -> 8.38 us  [the longest x2 4.67 us: reduce_two(): s = s + widen(first(narrow(g[i]), i))]
    unnamed x16 -> x31, local copies, waits for them, and re-layouts: 4.58 us -> 12 us
    psum x1, blocking collectives: 76.6 us -> 83.2 us  [body(): sums = lax.psum(jnp.sum(sums, axis=1), ('row', 'col'))]
  transfers between devices with their start and end apart: 4 -> 36, of which waited for: 2 -> 11; matrix products, arithmetic and copies ran while one was open for 5% -> 8% of each run, Pallas kernels for 0% -> 0%
where the time goes in v1:
time: 369 us; the launch traced here: 365 us
  blocking collectives  208 us (56%)
  starting transfers between devices  53.1 us (14%)
  waiting for transfers between devices  39.5 us (11%)
  other arithmetic  23.6 us (6%)
  Pallas kernels  23.3 us (6%)
  local copies, waits for them, and re-layouts  14.5 us (4%)
    unnamed x1, blocking collectives  125 us
    psum x1, blocking collectives, body(): sums = lax.psum(jnp.sum(sums, axis=1), ('row', 'col'))  83.2 us
    ppermute x26, starting transfers between devices, send_plane(): return lax.ppermute(x, 'col', pairs)  34.4 us
    pallas_call x1, Pallas kernels, pairs_block(): pl.pallas_call(lambda *refs: pair_kernel(own, total, *refs), grid=(rows /...  23.3 us
    ppermute x10, waiting for transfers between devices, send_z(): return lax.ppermute(x, 'row', [(i, (i + d) % NZ) for i in range(NZ)])  21.3 us
    ppermute x10, starting transfers between devices, send_z(): return lax.ppermute(x, 'row', [(i, (i + d) % NZ) for i in range(NZ)])  18.7 us
    ppermute x26, waiting for transfers between devices, send_plane(): return lax.ppermute(x, 'col', pairs)  18.2 us
    unnamed x31, local copies, waits for them, and re-layouts  12 us
  transfers between devices with their start and end apart: 36, of which 11 were waited for; matrix products, arithmetic and copies ran while one was open for 8% of the time, Pallas kernels for 0%

profile of v1, /device:TPU:32, one launch (start us, length us, event | category | flops | bytes accessed | tf_op | source)
XLA Modules:
  0.0 364.6 jit_solution(6557057958703536057)
XLA Ops:
  1.7 1.8 constant_dynamic-update-slice_fusion.19
  3.5 1.8 collective-permute-start.12
  8.3 3.0 collective-permute-start
  17.9 2.8 collective-permute-start.6
  25.3 6.4 %collective-permute-start.14 = (bf16[80,1152]{1,0:T(8,128)(2,1)}, bf16[80,1152]{1,0:T(8,128)(2,1)S(1)}, u32[]{:S(2)}, u32[]{:S(2)}) collective-permute-start(bf16[80,1152]{1,0:T(8,128)(2,1)} %get-tuple-element.16), channel_id=1, source_target_pairs={{0,128},{32,160},{64,192},{96,224},{128,0},{160,32},{192,64},{224,... | collective-permute-start | bytes 552968 | tf_op jit(solution)/shard_map/ppermute | solution.py:20
  31.7 2.4 collective-permute-start.3
  38.3 2.3 collective-permute-start.9
  40.5 1.7 collective-permute-start.10
  43.8 3.5 collective-permute-done.3
  47.3 1.9 collective-permute-start.11
  52.0 4.8 %collective-permute-done.15 = bf16[160,1152]{1,0:T(8,128)(2,1)S(1)} collective-permute-done((bf16[160,1152]{1,0:T(8,128)(2,1)S(1)}, bf16[160,1152]{1,0:T(8,128)(2,1)S(1)}, u32[]{:S(2)}, u32[]{:S(2)}) %collective-permute-start.15) | collective-permute-done | bytes 368672 | tf_op jit(solution)/shard_map/ppermute | solution.py:20
  57.8 2.1 collective-permute-done.16
  61.2 3.2 collective-permute-done.17
  66.2 23.3 %pair_block.1 = (f32[1280,1152]{1,0:T(8,128)}, f32[1280,1152]{1,0:T(8,128)}, f32[1280,1]{1,0:T(8,128)S(1)}, f32[2,1280]{1,0:T(2,128)S(1)}) custom-call(f32[2]{0:T(128)S(1)} %pad_maximum_fusion.6.refs_0_, bf16[1280,1152]{1,0:T(8,128)(2,1)S(1)} %constant_dynamic-update-slice_fusion.refs_1_, bf16[1280,1152]{1,0:T(8,128)(2,1)} %copy-done.1), custom_call_target="tpu_custom_call" | custom-call | tf_op jit(solution)/shard_map/pair_block/pallas_call | solution.py:114
  89.5 2.1 multiply_convert_fusion
  91.8 1.8 multiply_convert_fusion.6
  93.8 3.2 collective-permute-start.19
  98.8 83.2 %psum.7 = f32[2]{0:T(128)S(1)} all-reduce(f32[2]{0:T(128)S(1)} %reduce_sum.49), channel_id=1, replica_groups=mesh['row'=8,'col'=32] {'row','col'}, use_global_device_ids=true, to_apply=%region_6.8 | all-reduce | flops 2 | bytes 16 | tf_op jit(solution)/shard_map/psum | solution.py:165
  182.9 3.3 multiply_add_fusion.2
  188.0 2.7 collective-permute-start.22
  191.6 124.6 %all-reduce = f32[2560]{0:T(1024)S(1)} all-reduce(f32[2560]{0:T(1024)S(1)} %select_n.47), channel_id=2, replica_groups=mesh['row'=8,'col'=32] {'col'}, use_global_device_ids=true, to_apply=%region_2.4.clone | all-reduce | flops 2560 | bytes 20480
  316.8 3.2 collective-permute-start.26
  321.1 10.2 %collective-permute-done.24 = f16[160,1152]{1,0:T(8,128)(2,1)S(1)} collective-permute-done((f16[160,1152]{1,0:T(8,128)(2,1)}, f16[160,1152]{1,0:T(8,128)(2,1)S(1)}, u32[]{:S(2)}, u32[]{:S(2)}) %collective-permute-start.24) | collective-permute-done | bytes 368672 | tf_op jit(solution)/shard_map/ppermute | solution.py:31
  333.9 2.7 collective-permute-start.29
  336.7 2.6 multiply_add_fusion
  339.4 1.7 collective-permute-start.33
  341.9 6.2 %collective-permute-done.33 = f16[160,1152]{1,0:T(8,128)(2,1)S(1)} collective-permute-done((f16[160,1152]{1,0:T(8,128)(2,1)S(1)}, f16[160,1152]{1,0:T(8,128)(2,1)S(1)}, u32[]{:S(2)}, u32[]{:S(2)}) %collective-permute-start.33) | collective-permute-done | bytes 368672 | tf_op jit(solution)/shard_map/ppermute | solution.py:20
  348.2 1.6 collective-permute-done.31
  350.7 1.9 collective-permute-start.34
  352.6 3.5 collective-permute-start.35
  357.0 3.6 collective-permute-done.32
  360.5 2.9 collective-permute-done.35
  (119 shorter events, 39.8 us)
Async XLA Ops:
  3.5 33.9 %collective-permute-start.12 = (bf16[80,1152]{1,0:T(8,128)(2,1)}, bf16[80,1152]{1,0:T(8,128)(2,1)S(1)}, u32[]{:S(2)}, u32[]{:S(2)}) collective-permute-start(bf16[80,1152]{1,0:T(8,128)(2,1)} %get-tuple-element.16), channel_id=1, source_target_pairs={{0,224},{32,0},{64,32},{96,64},{128,96},{160,128},{192,160},{224,1... | collective-permute-start | bytes 552968 | tf_op jit(solution)/shard_map/ppermute | solution.py:20
  5.3 33.0 %collective-permute-start.13 = (bf16[80,1152]{1,0:T(8,128)(2,1)}, bf16[80,1152]{1,0:T(8,128)(2,1)S(1)}, u32[]{:S(2)}, u32[]{:S(2)}) collective-permute-start(bf16[80,1152]{1,0:T(8,128)(2,1)} %get-tuple-element.16), channel_id=1, source_target_pairs={{0,32},{32,64},{64,96},{96,128},{128,160},{160,192},{192,224},{224... | collective-permute-start | bytes 552968 | tf_op jit(solution)/shard_map/ppermute | solution.py:20
  8.3 9.6 %collective-permute-start = (bf16[40,1152]{1,0:T(8,128)(2,1)}, bf16[40,1152]{1,0:T(8,128)(2,1)}, u32[]{:S(2)}, u32[]{:S(2)}) collective-permute-start(bf16[40,1152]{1,0:T(8,128)(2,1)} %get-tuple-element.49), channel_id=1, source_target_pairs={{0,24},{1,25},{2,26},{3,27},{4,28},{5,29},{6,30},{7,31},{8,0},{9,1... | collective-permute-start | bytes 276488 | tf_op jit(solution)/shard_map/ppermute | solution.py:31
  11.3 10.2 %collective-permute-start.1 = (bf16[40,1152]{1,0:T(8,128)(2,1)}, bf16[40,1152]{1,0:T(8,128)(2,1)}, u32[]{:S(2)}, u32[]{:S(2)}) collective-permute-start(bf16[40,1152]{1,0:T(8,128)(2,1)} %get-tuple-element.49), channel_id=1, source_target_pairs={{0,16},{1,17},{2,18},{3,19},{4,20},{5,21},{6,22},{7,23},{8,24},{9,... | collective-permute-start | bytes 276488 | tf_op jit(solution)/shard_map/ppermute | solution.py:31
  11.9 10.5 %collective-permute-start.2 = (bf16[40,1152]{1,0:T(8,128)(2,1)}, bf16[40,1152]{1,0:T(8,128)(2,1)}, u32[]{:S(2)}, u32[]{:S(2)}) collective-permute-start(bf16[40,1152]{1,0:T(8,128)(2,1)} %get-tuple-element.49), channel_id=1, source_target_pairs={{0,8},{1,9},{2,10},{3,11},{4,12},{5,13},{6,14},{7,15},{8,16},{9,17... | collective-permute-start | bytes 276488 | tf_op jit(solution)/shard_map/ppermute | solution.py:31
  21.6 10.1 %collective-permute-start.7 = (bf16[40,1152]{1,0:T(8,128)(2,1)}, bf16[40,1152]{1,0:T(8,128)(2,1)S(1)}, u32[]{:S(2)}, u32[]{:S(2)}) collective-permute-start(bf16[40,1152]{1,0:T(8,128)(2,1)} %get-tuple-element.47), channel_id=1, source_target_pairs={{0,4},{1,5},{2,6},{3,7},{4,0},{5,1},{6,2},{7,3},{8,12},{9,13},{10,... | collective-permute-start | bytes 276488 | tf_op jit(solution)/shard_map/ppermute | solution.py:31
  22.5 11.6 %collective-permute-start.8 = (bf16[40,1152]{1,0:T(8,128)(2,1)}, bf16[40,1152]{1,0:T(8,128)(2,1)S(1)}, u32[]{:S(2)}, u32[]{:S(2)}) collective-permute-start(bf16[40,1152]{1,0:T(8,128)(2,1)} %get-tuple-element.47), channel_id=1, source_target_pairs={{0,2},{1,3},{2,4},{3,5},{4,6},{5,7},{6,0},{7,1},{8,10},{9,11},{10,... | collective-permute-start | bytes 276488 | tf_op jit(solution)/shard_map/ppermute | solution.py:31
  25.3 15.2 %collective-permute-start.14 = (bf16[80,1152]{1,0:T(8,128)(2,1)}, bf16[80,1152]{1,0:T(8,128)(2,1)S(1)}, u32[]{:S(2)}, u32[]{:S(2)}) collective-permute-start(bf16[80,1152]{1,0:T(8,128)(2,1)} %get-tuple-element.16), channel_id=1, source_target_pairs={{0,128},{32,160},{64,192},{96,224},{128,0},{160,32},{192,64},{224,... | collective-permute-start | bytes 552968 | tf_op jit(solution)/shard_map/ppermute | solution.py:20
  31.7 15.6 %collective-permute-start.3 = (bf16[160,1152]{1,0:T(8,128)(2,1)S(1)}, bf16[160,1152]{1,0:T(8,128)(2,1)S(1)}, u32[]{:S(2)}, u32[]{:S(2)}) collective-permute-start(bf16[160,1152]{1,0:T(8,128)(2,1)S(1)} %pad_maximum_fusion.2), channel_id=1, source_target_pairs={{0,6},{1,7},{2,0},{3,1},{4,2},{5,3},{6,4},{7,5},{8,14},{9,15},{10,... | collective-permute-start | bytes 1105928 | tf_op jit(solution)/shard_map/ppermute | solution.py:31
  34.1 15.2 %collective-permute-start.4 = (bf16[160,1152]{1,0:T(8,128)(2,1)S(1)}, bf16[160,1152]{1,0:T(8,128)(2,1)S(1)}, u32[]{:S(2)}, u32[]{:S(2)}) collective-permute-start(bf16[160,1152]{1,0:T(8,128)(2,1)S(1)} %pad_maximum_fusion.2), channel_id=1, source_target_pairs={{0,4},{1,5},{2,6},{3,7},{4,0},{5,1},{6,2},{7,3},{8,12},{9,13},{10,... | collective-permute-start | bytes 1105928 | tf_op jit(solution)/shard_map/ppermute | solution.py:31
  37.4 13.6 %collective-permute-start.5 = (bf16[160,1152]{1,0:T(8,128)(2,1)S(1)}, bf16[160,1152]{1,0:T(8,128)(2,1)S(1)}, u32[]{:S(2)}, u32[]{:S(2)}) collective-permute-start(bf16[160,1152]{1,0:T(8,128)(2,1)S(1)} %pad_maximum_fusion.2), channel_id=1, source_target_pairs={{0,2},{1,3},{2,4},{3,5},{4,6},{5,7},{6,0},{7,1},{8,10},{9,11},{10,... | collective-permute-start | bytes 1105928 | tf_op jit(solution)/shard_map/ppermute | solution.py:31
  38.3 22.7 %collective-permute-start.9 = (bf16[160,1152]{1,0:T(8,128)(2,1)S(1)}, bf16[160,1152]{1,0:T(8,128)(2,1)S(1)}, u32[]{:S(2)}, u32[]{:S(2)}) collective-permute-start(bf16[160,1152]{1,0:T(8,128)(2,1)S(1)} %pad_maximum_fusion.3), channel_id=1, source_target_pairs={{0,24},{1,25},{2,26},{3,27},{4,28},{5,29},{6,30},{7,31},{8,0},{9,1... | collective-permute-start | bytes 1105928 | tf_op jit(solution)/shard_map/ppermute | solution.py:31
  40.5 20.5 %collective-permute-start.10 = (bf16[160,1152]{1,0:T(8,128)(2,1)S(1)}, bf16[160,1152]{1,0:T(8,128)(2,1)S(1)}, u32[]{:S(2)}, u32[]{:S(2)}) collective-permute-start(bf16[160,1152]{1,0:T(8,128)(2,1)S(1)} %pad_maximum_fusion.3), channel_id=1, source_target_pairs={{0,16},{1,17},{2,18},{3,19},{4,20},{5,21},{6,22},{7,23},{8,24},{9,... | collective-permute-start | bytes 1105928 | tf_op jit(solution)/shard_map/ppermute | solution.py:31
  47.3 13.8 %collective-permute-start.11 = (bf16[160,1152]{1,0:T(8,128)(2,1)S(1)}, bf16[160,1152]{1,0:T(8,128)(2,1)S(1)}, u32[]{:S(2)}, u32[]{:S(2)}) collective-permute-start(bf16[160,1152]{1,0:T(8,128)(2,1)S(1)} %pad_maximum_fusion.3), channel_id=1, source_target_pairs={{0,8},{1,9},{2,10},{3,11},{4,12},{5,13},{6,14},{7,15},{8,16},{9,17... | collective-permute-start | bytes 1105928 | tf_op jit(solution)/shard_map/ppermute | solution.py:31
  51.0 9.0 %collective-permute-start.16 = (bf16[160,1152]{1,0:T(8,128)(2,1)S(1)}, bf16[160,1152]{1,0:T(8,128)(2,1)S(1)}, u32[]{:S(2)}, u32[]{:S(2)}) collective-permute-start(bf16[160,1152]{1,0:T(8,128)(2,1)S(1)} %get-tuple-element.45), channel_id=1, source_target_pairs={{0,32},{32,64},{64,96},{96,128},{128,160},{160,192},{192,224},{224... | collective-permute-start | bytes 1105928 | tf_op jit(solution)/shard_map/ppermute | solution.py:20
  91.6 245.0 %collective-permute-start.30 = (f16[640,1152]{1,0:T(8,128)(2,1)S(1)}, f16[640,1152]{1,0:T(8,128)(2,1)}, u32[]{:S(2)}, u32[]{:S(2)}) collective-permute-start(f16[640,1152]{1,0:T(8,128)(2,1)S(1)} %multiply_convert_fusion), channel_id=1, source_target_pairs={{0,1},{1,0},{2,3},{3,2},{4,5},{5,4},{6,7},{7,6},{8,9},{9,8},{10,11... | collective-permute-start | bytes 4423688 | tf_op jit(solution)/shard_map/ppermute | solution.py:31
  93.6 88.6 %collective-permute-start.18 = (f16[160,1152]{1,0:T(8,128)(2,1)S(1)}, f16[160,1152]{1,0:T(8,128)(2,1)S(1)}, u32[]{:S(2)}, u32[]{:S(2)}) collective-permute-start(f16[160,1152]{1,0:T(8,128)(2,1)S(1)} %get-tuple-element.21), channel_id=1, source_target_pairs={{0,2},{1,3},{2,4},{3,5},{4,6},{5,7},{6,0},{7,1},{8,10},{9,11},{10,... | collective-permute-start | bytes 1105928 | tf_op jit(solution)/shard_map/ppermute | solution.py:31
  93.8 88.4 %collective-permute-start.19 = (f16[160,1152]{1,0:T(8,128)(2,1)S(1)}, f16[160,1152]{1,0:T(8,128)(2,1)S(1)}, u32[]{:S(2)}, u32[]{:S(2)}) collective-permute-start(f16[160,1152]{1,0:T(8,128)(2,1)S(1)} %get-tuple-element.23), channel_id=1, source_target_pairs={{0,4},{1,5},{2,6},{3,7},{4,0},{5,1},{6,2},{7,3},{8,12},{9,13},{10,... | collective-permute-start | bytes 1105928 | tf_op jit(solution)/shard_map/ppermute | solution.py:31
  97.0 85.9 %collective-permute-start.20 = (f16[160,1152]{1,0:T(8,128)(2,1)S(1)}, f16[160,1152]{1,0:T(8,128)(2,1)}, u32[]{:S(2)}, u32[]{:S(2)}) collective-permute-start(f16[160,1152]{1,0:T(8,128)(2,1)S(1)} %get-tuple-element.22), channel_id=1, source_target_pairs={{0,6},{1,7},{2,0},{3,1},{4,2},{5,3},{6,4},{7,5},{8,14},{9,15},{10,... | collective-permute-start | bytes 1105928 | tf_op jit(solution)/shard_map/ppermute | solution.py:31
  187.0 129.8 %collective-permute-start.21 = (f16[40,1152]{1,0:T(8,128)(2,1)S(1)}, f16[40,1152]{1,0:T(8,128)(2,1)S(1)}, u32[]{:S(2)}, u32[]{:S(2)}) collective-permute-start(f16[40,1152]{1,0:T(8,128)(2,1)S(1)} %get-tuple-element.29), channel_id=1, source_target_pairs={{0,8},{1,9},{2,10},{3,11},{4,12},{5,13},{6,14},{7,15},{8,16},{9,17... | collective-permute-start | bytes 276488 | tf_op jit(solution)/shard_map/ppermute | solution.py:31
  188.0 128.9 %collective-permute-start.22 = (f16[40,1152]{1,0:T(8,128)(2,1)}, f16[40,1152]{1,0:T(8,128)(2,1)}, u32[]{:S(2)}, u32[]{:S(2)}) collective-permute-start(f16[40,1152]{1,0:T(8,128)(2,1)} %get-tuple-element.31), channel_id=1, source_target_pairs={{0,16},{1,17},{2,18},{3,19},{4,20},{5,21},{6,22},{7,23},{8,24},{9,... | collective-permute-start | bytes 276488 | tf_op jit(solution)/shard_map/ppermute | solution.py:31
  190.7 129.3 %collective-permute-start.23 = (f16[40,1152]{1,0:T(8,128)(2,1)}, f16[40,1152]{1,0:T(8,128)(2,1)}, u32[]{:S(2)}, u32[]{:S(2)}) collective-permute-start(f16[40,1152]{1,0:T(8,128)(2,1)} %get-tuple-element.30), channel_id=1, source_target_pairs={{0,24},{1,25},{2,26},{3,27},{4,28},{5,29},{6,30},{7,31},{8,0},{9,1... | collective-permute-start | bytes 276488 | tf_op jit(solution)/shard_map/ppermute | solution.py:31
  316.7 14.6 %collective-permute-start.24 = (f16[160,1152]{1,0:T(8,128)(2,1)}, f16[160,1152]{1,0:T(8,128)(2,1)S(1)}, u32[]{:S(2)}, u32[]{:S(2)}) collective-permute-start(f16[160,1152]{1,0:T(8,128)(2,1)} %get-tuple-element.20), channel_id=1, source_target_pairs={{0,8},{1,9},{2,10},{3,11},{4,12},{5,13},{6,14},{7,15},{8,16},{9,17... | collective-permute-start | bytes 1105928 | tf_op jit(solution)/shard_map/ppermute | solution.py:31
  316.7 14.6 %collective-permute-start.25 = (f16[160,1152]{1,0:T(8,128)(2,1)}, f16[160,1152]{1,0:T(8,128)(2,1)S(1)}, u32[]{:S(2)}, u32[]{:S(2)}) collective-permute-start(f16[160,1152]{1,0:T(8,128)(2,1)} %get-tuple-element.19), channel_id=1, source_target_pairs={{0,16},{1,17},{2,18},{3,19},{4,20},{5,21},{6,22},{7,23},{8,24},{9,... | collective-permute-start | bytes 1105928 | tf_op jit(solution)/shard_map/ppermute | solution.py:31
  316.8 15.1 %collective-permute-start.26 = (f16[160,1152]{1,0:T(8,128)(2,1)S(1)}, f16[160,1152]{1,0:T(8,128)(2,1)S(1)}, u32[]{:S(2)}, u32[]{:S(2)}) collective-permute-start(f16[160,1152]{1,0:T(8,128)(2,1)S(1)} %get-tuple-element.18), channel_id=1, source_target_pairs={{0,24},{1,25},{2,26},{3,27},{4,28},{5,29},{6,30},{7,31},{8,0},{9,1... | collective-permute-start | bytes 1105928 | tf_op jit(solution)/shard_map/ppermute | solution.py:31
  333.3 7.7 %collective-permute-start.27 = (f16[40,1152]{1,0:T(8,128)(2,1)S(1)}, f16[40,1152]{1,0:T(8,128)(2,1)S(1)}, u32[]{:S(2)}, u32[]{:S(2)}) collective-permute-start(f16[40,1152]{1,0:T(8,128)(2,1)S(1)} %get-tuple-element.32), channel_id=1, source_target_pairs={{0,2},{1,3},{2,4},{3,5},{4,6},{5,7},{6,0},{7,1},{8,10},{9,11},{10,... | collective-permute-start | bytes 276488 | tf_op jit(solution)/shard_map/ppermute | solution.py:31
  333.4 7.6 %collective-permute-start.28 = (f16[40,1152]{1,0:T(8,128)(2,1)S(1)}, f16[40,1152]{1,0:T(8,128)(2,1)S(1)}, u32[]{:S(2)}, u32[]{:S(2)}) collective-permute-start(f16[40,1152]{1,0:T(8,128)(2,1)S(1)} %get-tuple-element.34), channel_id=1, source_target_pairs={{0,4},{1,5},{2,6},{3,7},{4,0},{5,1},{6,2},{7,3},{8,12},{9,13},{10,... | collective-permute-start | bytes 276488 | tf_op jit(solution)/shard_map/ppermute | solution.py:31
  339.4 8.7 %collective-permute-start.33 = (f16[160,1152]{1,0:T(8,128)(2,1)S(1)}, f16[160,1152]{1,0:T(8,128)(2,1)S(1)}, u32[]{:S(2)}, u32[]{:S(2)}) collective-permute-start(f16[160,1152]{1,0:T(8,128)(2,1)S(1)} %get-tuple-element.28), channel_id=1, source_target_pairs={{0,224},{32,0},{64,32},{96,64},{128,96},{160,128},{192,160},{224,1... | collective-permute-start | bytes 1105928 | tf_op jit(solution)/shard_map/ppermute | solution.py:20
  341.4 8.5 %collective-permute-start.31 = (f16[160,1152]{1,0:T(8,128)(2,1)S(1)}, f16[160,1152]{1,0:T(8,128)(2,1)S(1)}, u32[]{:S(2)}, u32[]{:S(2)}) collective-permute-start(f16[160,1152]{1,0:T(8,128)(2,1)S(1)} %get-tuple-element.27), channel_id=1, source_target_pairs={{0,32},{32,64},{64,96},{96,128},{128,160},{160,192},{192,224},{224... | collective-permute-start | bytes 1105928 | tf_op jit(solution)/shard_map/ppermute | solution.py:20
  350.1 10.4 %collective-permute-start.32 = (f16[80,1152]{1,0:T(8,128)(2,1)S(1)}, f16[80,1152]{1,0:T(8,128)(2,1)S(1)}, u32[]{:S(2)}, u32[]{:S(2)}) collective-permute-start(f16[80,1152]{1,0:T(8,128)(2,1)S(1)} %get-tuple-element.24), channel_id=1, source_target_pairs={{0,32},{32,64},{64,96},{96,128},{128,160},{160,192},{192,224},{224... | collective-permute-start | bytes 552968 | tf_op jit(solution)/shard_map/ppermute | solution.py:20
  350.7 9.9 %collective-permute-start.34 = (f16[80,1152]{1,0:T(8,128)(2,1)S(1)}, f16[80,1152]{1,0:T(8,128)(2,1)S(1)}, u32[]{:S(2)}, u32[]{:S(2)}) collective-permute-start(f16[80,1152]{1,0:T(8,128)(2,1)S(1)} %get-tuple-element.26), channel_id=1, source_target_pairs={{0,224},{32,0},{64,32},{96,64},{128,96},{160,128},{192,160},{224,1... | collective-permute-start | bytes 552968 | tf_op jit(solution)/shard_map/ppermute | solution.py:20
  352.6 10.8 %collective-permute-start.35 = (f16[80,1152]{1,0:T(8,128)(2,1)S(1)}, f16[80,1152]{1,0:T(8,128)(2,1)S(1)}, u32[]{:S(2)}, u32[]{:S(2)}) collective-permute-start(f16[80,1152]{1,0:T(8,128)(2,1)S(1)} %get-tuple-element.25), channel_id=1, source_target_pairs={{0,128},{32,160},{64,192},{96,224},{128,0},{160,32},{192,64},{224,... | collective-permute-start | bytes 552968 | tf_op jit(solution)/shard_map/ppermute | solution.py:20
  (10 other events, 58.8 us)
